TPU v7x, 32 devices: a whole 2x2x4 slice. The times are simulated.
32 devices in a mesh: groups: 2 (over x), samples: 16 (over z, y, core).
Axes of the slice: x: 2, y: 2, z: 4, core: 2. Of those that a mesh axis runs over, the one named last changes fastest.
Arguments:
- energies: float32 [256, 393216], P(None, ('groups', 'samples')), parts along dimension 1, may hold values from -700 to 700
- mult: int32 [393216, 256], P(('groups', 'samples')), parts along dimension 0, may hold values from 0 to 3
- state_counts: int32 [512], P('groups'), parts along dimension 0, may hold values from 1 to 1536, 196608 in all
Outputs:
- free_energy: float32 [512, 256], P('groups'), parts along dimension 0
There are 2 independent parts, one for each index of `groups`. A program takes and returns all parts, laid end to end along the dimension named above; each array names one. Nothing has to cross between parts.
All inputs are finite; a program needn't handle non-finite values.
Results may differ from a plain program's by a relative error of at most 0.0003.
Values sent between devices are 32-bit elements; how exact they have to be, the bound alone decides.
A program may use at most 128 MiB of HBM per device.

v0:
```python
import jax
import jax.numpy as jnp
from jax import lax
from jax.sharding import PartitionSpec as P

ITERS = 4


def weighted_terms(boltz, weight, mult_part):
    denom = lax.dot_general(
        boltz, weight, (((0,), (0,)), ((), ())), preferred_element_type=jnp.float32
    )
    ratio = (mult_part.astype(jnp.float32) / denom).astype(jnp.bfloat16)
    return jnp.dot(boltz, ratio, preferred_element_type=jnp.float32)


def settle(partial_sums):
    totals = lax.psum(partial_sums, "samples")
    logs = jnp.log(totals)
    return logs[0:1] - logs


def on_device(energies, mult, state_counts):
    shift = jnp.min(energies, axis=0, keepdims=True)
    boltz = jnp.exp(shift - energies).astype(jnp.bfloat16)
    counts_f = state_counts.astype(jnp.float32)[:, None]
    num_states = energies.shape[0]
    num_reps = mult.shape[1]
    free = jnp.zeros((num_states, num_reps), jnp.float32)
    for step in range(ITERS):
        weight = (counts_f * jnp.exp(free)).astype(jnp.bfloat16)
        free = settle(weighted_terms(boltz, weight, mult))
    return free


def solution(mesh):
    in_specs = (P(None, ("groups", "samples")), P(("groups", "samples"), None), P("groups"))
    out_specs = P("groups", None)
    return jax.shard_map(
        on_device, mesh=mesh, in_specs=in_specs, out_specs=out_specs, check_vma=False
    )
```

profile of v0, /device:TPU:1, one launch (start us, length us, event | category | flops | bytes accessed | tf_op | source)
XLA Modules:
  0.0 444.2 jit_solution(2489789016998661210)
XLA Ops:
  6.5 0.0 all-reduce.5.cloned.1.call-start
  6.5 0.7 fusion.24
  7.2 5.2 %reduce_min.9 = f32[12288]{0:T(1024)S(1)} reduce(f32[256,12288]{1,0:T(8,128)} %param.3, f32[]{:T(128)} %constant.0.clone.1), dimensions={0}, to_apply=%region_0.0 | reduce | flops 3133440 | bytes 12632068 | tf_op jit(solution)/shard_map/reduce_min | solution.py:24
  12.4 9.0 %exponential_convert_fusion = bf16[256,12288]{1,0:T(8,128)(2,1)} fusion(f32[256,12288]{1,0:T(8,128)} %param.3, f32[12288]{0:T(1024)S(1)} %reduce_min.9), kind=kLoop, calls=%fused_computation.4 | loop fusion | flops 6291456 | bytes 18923520 | tf_op jit(solution)/shard_map/convert_element_type | solution.py:25
  21.4 12.6 %fusion = f32[256,256]{1,0:T(8,128)} fusion(bf16[256,12288]{1,0:T(8,128)(2,1)} %exponential_convert_fusion, s32[12288,256]{1,0:T(8,128)} %param.4, bf16[256]{0:T(256)(128)(2,1)S(1)} %get-tuple-element.6), kind=kOutput, calls=%fused_computation.5 | convolution fusion | flops 3230662656 | bytes 19137024 | tf_op jit(solution)/shard_map/dot_general | solution.py:14
  34.0 0.0 all-reduce.5.cloned.1.call-update
  34.0 0.0 all-reduce.7.cloned.1.call-start
  34.0 91.6 %all-reduce.5.cloned.1.call-done = f32[256,256]{1,0:T(8,128)} async-done(((f32[256,256]{1,0:T(8,128)}), f32[256,256]{1,0:T(8,128)}) %all-reduce.5.cloned.1.call-update) | async-done | bytes 262160 | tf_op jit(solution)/shard_map/psum | solution.py:18
  125.6 1.0 log.12
  126.6 12.7 %fusion.1 = f32[256,256]{1,0:T(8,128)} fusion(bf16[256,12288]{1,0:T(8,128)(2,1)} %exponential_convert_fusion, s32[12288,256]{1,0:T(8,128)} %param.4, f32[256]{0:T(256)S(1)} %bitcast.14, f32[256]{0:T(256)S(1)} %get-tuple-element.5, f32[256,256]{1,0:T(8,128)} %all-reduce.5.cloned.1.call-done), kind=kOutput, calls=%fused_computation.6 | convolution fusion | flops 3230859264 | bytes 19400704 | tf_op jit(solution)/shard_map/dot_general | solution.py:14
  139.3 0.0 all-reduce.7.cloned.1.call-update
  139.3 0.2 all-reduce.9.cloned.1.call-start
  139.5 89.2 %all-reduce.7.cloned.1.call-done = f32[256,256]{1,0:T(8,128)} async-done(((f32[256,256]{1,0:T(8,128)}), f32[256,256]{1,0:T(8,128)}) %all-reduce.7.cloned.1.call-update) | async-done | bytes 262160 | tf_op jit(solution)/shard_map/psum | solution.py:18
  228.7 1.0 log.13
  229.7 12.7 %fusion.2 = f32[256,256]{1,0:T(8,128)} fusion(bf16[256,12288]{1,0:T(8,128)(2,1)} %exponential_convert_fusion, s32[12288,256]{1,0:T(8,128)} %param.4, f32[256]{0:T(256)S(1)} %bitcast.15, f32[256]{0:T(256)S(1)} %get-tuple-element.5, f32[256,256]{1,0:T(8,128)} %all-reduce.7.cloned.1.call-done), kind=kOutput, calls=%fused_computation.7 | convolution fusion | flops 3230859264 | bytes 19400704 | tf_op jit(solution)/shard_map/dot_general | solution.py:14
  242.4 0.0 all-reduce.9.cloned.1.call-update
  242.4 0.0 all-reduce.11.cloned.1.call-start
  242.5 89.4 %all-reduce.9.cloned.1.call-done = f32[256,256]{1,0:T(8,128)} async-done(((f32[256,256]{1,0:T(8,128)}), f32[256,256]{1,0:T(8,128)}) %all-reduce.9.cloned.1.call-update) | async-done | bytes 262160 | tf_op jit(solution)/shard_map/psum | solution.py:18
  331.8 1.0 log.14
  332.8 12.7 %fusion.3 = f32[256,256]{1,0:T(8,128)} fusion(bf16[256,12288]{1,0:T(8,128)(2,1)} %exponential_convert_fusion, s32[12288,256]{1,0:T(8,128)} %param.4, f32[256]{0:T(256)S(1)} %bitcast.13, f32[256]{0:T(256)S(1)} %get-tuple-element.5, f32[256,256]{1,0:T(8,128)} %all-reduce.9.cloned.1.call-done), kind=kOutput, calls=%fused_computation.8 | convolution fusion | flops 3230859264 | bytes 19400704 | tf_op jit(solution)/shard_map/dot_general | solution.py:14
  345.5 0.0 all-reduce.11.cloned.1.call-update
  345.5 89.4 %all-reduce.11.cloned.1.call-done = f32[256,256]{1,0:T(8,128)} async-done(((f32[256,256]{1,0:T(8,128)}), f32[256,256]{1,0:T(8,128)}) %all-reduce.11.cloned.1.call-update) | async-done | bytes 262160 | tf_op jit(solution)/shard_map/psum | solution.py:18
  435.0 1.0 log.15
  436.0 1.7 broadcast_subtract_fusion
  (4 shorter events, 0.0 us)
Async XLA Ops:
  6.5 119.1 %all-reduce.5.cloned.1.call-start = ((), (), s32[]{:S(2)}) async-start(), calls=%async_computation | async-start | bytes 524288 | tf_op jit(solution)/shard_map/psum | solution.py:18
  34.0 194.7 %all-reduce.7.cloned.1.call-start = ((), (), s32[]{:S(2)}) async-start(), calls=%async_computation.1 | async-start | bytes 524288 | tf_op jit(solution)/shard_map/psum | solution.py:18
  139.3 192.5 %all-reduce.9.cloned.1.call-start = ((), (), s32[]{:S(2)}) async-start(), calls=%async_computation.2 | async-start | bytes 524288 | tf_op jit(solution)/shard_map/psum | solution.py:18
  242.4 192.5 %all-reduce.11.cloned.1.call-start = ((), (), s32[]{:S(2)}) async-start(), calls=%async_computation.3 | async-start | bytes 524288 | tf_op jit(solution)/shard_map/psum | solution.py:18
Sparse Core Ops, SparseCore 0:
  34.1 91.4 all-reduce.4
  139.4 89.2 all-reduce.6
  242.5 89.2 all-reduce.8
  345.6 89.2 all-reduce.10
where the time goes:
time: 445 us; the launch traced here: 444 us
  waiting for transfers between devices  360 us (81%)
  matrix products  50.5 us (11%)
  other arithmetic  16.5 us (4%)
  between operations  13.2 us (3%)
    psum x4, waiting for transfers between devices, settle(): totals = lax.psum(partial_sums, 'samples')  360 us
    dot_general x4, matrix products, weighted_terms(): return jnp.dot(boltz, ratio, preferred_element_type=jnp.float32)  50.5 us
    convert_element_type x1, other arithmetic, on_device(): boltz = jnp.exp(shift - energies).astype(jnp.bfloat16)  8.95 us
  transfers between devices with their start and end apart: 4, of which 4 were waited for; matrix products, arithmetic and copies ran while one was open for 0% of the time, Pallas kernels for 0%

commit v1 on v0

--- a/solution.py
+++ b/solution.py
@@ -15,7 +15,7 @@
 
 
 def settle(partial_sums):
-    totals = lax.psum(partial_sums, "samples")
+    totals = jnp.sum(lax.all_gather(partial_sums, "samples"), axis=0)
     logs = jnp.log(totals)
     return logs[0:1] - logs
 

time: 445 us -> 291 us (0.65)
  waiting for transfers between devices: 360 us -> 201 us
  other arithmetic: 16.5 us -> 25.5 us
    psum x4 -> x0, waiting for transfers between devices: 360 us -> none  [settle(): totals = lax.psum(partial_sums, 'samples')]
    all_gather x0 -> x4, waiting for transfers between devices: none -> 201 us  [settle(): totals = jnp.sum(lax.all_gather(partial_sums, 'samples'), axis=0)]
    reduce_sum x0 -> x4, other arithmetic: none -> 9.9 us  [settle(): totals = jnp.sum(lax.all_gather(partial_sums, 'samples'), axis=0)]
where the time goes in v1:
time: 291 us; the launch traced here: 290 us
  waiting for transfers between devices  201 us (69%)
  matrix products  50.3 us (17%)
  other arithmetic  25.5 us (9%)
  between operations  13.2 us (5%)
    all_gather x4, waiting for transfers between devices, settle(): totals = jnp.sum(lax.all_gather(partial_sums, 'samples'), axis=0)  201 us
    dot_general x4, matrix products, weighted_terms(): return jnp.dot(boltz, ratio, preferred_element_type=jnp.float32)  50.3 us
    reduce_sum x4, other arithmetic, settle(): totals = jnp.sum(lax.all_gather(partial_sums, 'samples'), axis=0)  9.9 us
    convert_element_type x1, other arithmetic, on_device(): boltz = jnp.exp(shift - energies).astype(jnp.bfloat16)  8.95 us
  transfers between devices with their start and end apart: 4, of which 4 were waited for; matrix products, arithmetic and copies ran while one was open for 0% of the time, Pallas kernels for 0%

profile of v1, /device:TPU:1, one launch (start us, length us, event | category | flops | bytes accessed | tf_op | source)
XLA Modules:
  0.0 290.1 jit_solution(13230520642509794378)
XLA Ops:
  6.5 0.0 all-gather.9.cloned.1.call-start
  6.5 0.7 fusion.24
  7.2 5.2 %reduce_min.9 = f32[12288]{0:T(1024)S(1)} reduce(f32[256,12288]{1,0:T(8,128)} %param.3, f32[]{:T(128)} %constant.0.clone.1), dimensions={0}, to_apply=%region_0.0 | reduce | flops 3133440 | bytes 12632068 | tf_op jit(solution)/shard_map/reduce_min | solution.py:24
  12.4 9.0 %exponential_convert_fusion = bf16[256,12288]{1,0:T(8,128)(2,1)} fusion(f32[256,12288]{1,0:T(8,128)} %param.3, f32[12288]{0:T(1024)S(1)} %reduce_min.9), kind=kLoop, calls=%fused_computation.4 | loop fusion | flops 6291456 | bytes 18923520 | tf_op jit(solution)/shard_map/convert_element_type | solution.py:25
  21.4 12.6 %fusion = f32[256,256]{1,0:T(8,128)} fusion(bf16[256,12288]{1,0:T(8,128)(2,1)} %exponential_convert_fusion, s32[12288,256]{1,0:T(8,128)} %param.4, bf16[256]{0:T(256)(128)(2,1)S(1)} %get-tuple-element.6), kind=kOutput, calls=%fused_computation.5 | convolution fusion | flops 3230662656 | bytes 19137024 | tf_op jit(solution)/shard_map/dot_general | solution.py:14
  34.0 0.0 all-gather.9.cloned.1.call-update
  34.0 0.0 all-gather.11.cloned.1.call-start
  34.0 53.2 %all-gather.9.cloned.1.call-done = f32[4096,256]{1,0:T(8,128)} async-done(((f32[256,256]{1,0:T(8,128)}), f32[4096,256]{1,0:T(8,128)}) %all-gather.9.cloned.1.call-update) | async-done | bytes 4194320 | tf_op jit(solution)/shard_map/all_gather | solution.py:18
  87.2 2.5 reduce_sum.36
  89.7 12.6 %fusion.1 = f32[256,256]{1,0:T(8,128)} fusion(bf16[256,12288]{1,0:T(8,128)(2,1)} %exponential_convert_fusion, s32[12288,256]{1,0:T(8,128)} %param.4, f32[256]{0:T(256)S(1)} %bitcast.22, f32[256]{0:T(256)S(1)} %get-tuple-element.5, f32[256,256]{1,0:T(8,128)S(1)} %reduce_sum.36), kind=kOutput, calls=%fused_computation.6 | convolution fusion | flops 3230859264 | bytes 19400704 | tf_op jit(solution)/shard_map/dot_general | solution.py:14
  102.3 0.0 all-gather.11.cloned.1.call-update
  102.3 0.2 all-gather.13.cloned.1.call-start
  102.6 49.0 %all-gather.11.cloned.1.call-done = f32[4096,256]{1,0:T(8,128)} async-done(((f32[256,256]{1,0:T(8,128)}), f32[4096,256]{1,0:T(8,128)}) %all-gather.11.cloned.1.call-update) | async-done | bytes 4194320 | tf_op jit(solution)/shard_map/all_gather | solution.py:18
  151.6 2.5 reduce_sum.37
  154.1 12.6 %fusion.2 = f32[256,256]{1,0:T(8,128)} fusion(bf16[256,12288]{1,0:T(8,128)(2,1)} %exponential_convert_fusion, s32[12288,256]{1,0:T(8,128)} %param.4, f32[256]{0:T(256)S(1)} %bitcast.23, f32[256]{0:T(256)S(1)} %get-tuple-element.5, f32[256,256]{1,0:T(8,128)S(1)} %reduce_sum.37), kind=kOutput, calls=%fused_computation.7 | convolution fusion | flops 3230859264 | bytes 19400704 | tf_op jit(solution)/shard_map/dot_general | solution.py:14
  166.7 0.0 all-gather.13.cloned.1.call-update
  166.7 0.0 all-gather.15.cloned.1.call-start
  166.8 49.2 %all-gather.13.cloned.1.call-done = f32[4096,256]{1,0:T(8,128)} async-done(((f32[256,256]{1,0:T(8,128)}), f32[4096,256]{1,0:T(8,128)}) %all-gather.13.cloned.1.call-update) | async-done | bytes 4194320 | tf_op jit(solution)/shard_map/all_gather | solution.py:18
  215.9 2.5 reduce_sum.38
  218.5 12.6 %fusion.3 = f32[256,256]{1,0:T(8,128)} fusion(bf16[256,12288]{1,0:T(8,128)(2,1)} %exponential_convert_fusion, s32[12288,256]{1,0:T(8,128)} %param.4, f32[256]{0:T(256)S(1)} %bitcast.21, f32[256]{0:T(256)S(1)} %get-tuple-element.5, f32[256,256]{1,0:T(8,128)S(1)} %reduce_sum.38), kind=kOutput, calls=%fused_computation.8 | convolution fusion | flops 3230859264 | bytes 19400704 | tf_op jit(solution)/shard_map/dot_general | solution.py:14
  231.0 0.0 all-gather.15.cloned.1.call-update
  231.1 49.2 %all-gather.15.cloned.1.call-done = f32[4096,256]{1,0:T(8,128)} async-done(((f32[256,256]{1,0:T(8,128)}), f32[4096,256]{1,0:T(8,128)}) %all-gather.15.cloned.1.call-update) | async-done | bytes 4194320 | tf_op jit(solution)/shard_map/all_gather | solution.py:18
  280.3 2.5 reduce_sum.39
  282.8 0.7 broadcast_subtract_fusion
  (8 shorter events, 0.2 us)
Async XLA Ops:
  6.5 80.7 %all-gather.9.cloned.1.call-start = ((), (), s32[]{:S(2)}) async-start(), calls=%async_computation | async-start | bytes 4456448 | tf_op jit(solution)/shard_map/all_gather | solution.py:18
  34.0 117.6 %all-gather.11.cloned.1.call-start = ((), (), s32[]{:S(2)}) async-start(), calls=%async_computation.1 | async-start | bytes 4456448 | tf_op jit(solution)/shard_map/all_gather | solution.py:18
  102.3 113.6 %all-gather.13.cloned.1.call-start = ((), (), s32[]{:S(2)}) async-start(), calls=%async_computation.2 | async-start | bytes 4456448 | tf_op jit(solution)/shard_map/all_gather | solution.py:18
  166.7 113.6 %all-gather.15.cloned.1.call-start = ((), (), s32[]{:S(2)}) async-start(), calls=%async_computation.3 | async-start | bytes 4456448 | tf_op jit(solution)/shard_map/all_gather | solution.py:18
Sparse Core Ops, SparseCore 0:
  34.1 53.0 all-gather.8
  102.5 49.0 all-gather.10
  166.8 49.0 all-gather.12
  231.2 49.0 all-gather.14
